TPU v7x, 32 devices: a whole 2x2x4 slice. The times are simulated.
32 devices in a mesh: grp: 2 (over x), exp: 4 (over y, core), base: 4 (over z).
Axes of the slice: x: 2, y: 2, z: 4, core: 2. Of those that a mesh axis runs over, the one named last changes fastest.
Arguments:
- tokens: bfloat16 [512, 7168], P(('grp', 'exp'), 'base'), parts along dimension 0, may hold values from -6 to 6
- expert_ids: int32 [512, 8], P(('grp', 'exp')), parts along dimension 0, may hold values from 0 to 15, all different within a row; in each aligned block of 64 rows (0 to 63, 64 to 127, ...) at most 48 rows name the same one
- gate_q: int32 [512, 8], P(('grp', 'exp')), parts along dimension 0, may hold values from 1 to 65536
- importance: float32 [7168], P('base'), may hold values from 0.5 to 18
- dense_gate: bfloat16 [16, 7168, 1024], P('exp', None, 'base'), may hold values from -0.0625 to 0.0625
- dense_up: bfloat16 [16, 7168, 1024], P('exp', None, 'base'), may hold values from -0.0625 to 0.0625
- dense_down: bfloat16 [16, 1024, 7168], P('exp', None, 'base'), may hold values from -0.1875 to 0.1875
- delta_gate: bfloat16 [16, 7168, 128], P('exp', None, 'base'), may hold values from -0.0625 to 0.0625
- delta_up: bfloat16 [16, 7168, 128], P('exp', None, 'base'), may hold values from -0.0625 to 0.0625
- delta_down: bfloat16 [16, 128, 7168], P('exp', None, 'base'), may hold values from -0.5 to 0.5
- base_gate: bfloat16 [7168, 1024], P(None, 'base'), may hold values from -0.0625 to 0.0625
- base_up: bfloat16 [7168, 1024], P(None, 'base'), may hold values from -0.0625 to 0.0625
- base_down: bfloat16 [1024, 7168], P('base'), may hold values from -0.1875 to 0.1875
Outputs:
- errors: float32 [512], P(('grp', 'exp')), parts along dimension 0
There are 2 independent parts, one for each index of `grp`. A program takes and returns all parts, laid end to end along the dimension named above; an argument that names none is the same for every part. Nothing has to cross between parts.
Inputs may be any that keep to these rules, and one draw needn't show every extreme that they name: `expert_ids`: A token names 8 different experts; among the tokens of one index of exp no expert is named more than 48 times.
All inputs are finite; a program needn't handle non-finite values.
Results may differ from a plain program's by a relative error of at most 0.00064.
Values may be sent and summed in bfloat16 or wider, within the bound.
A program may use at most 256 MiB of HBM per device.

v0:
```python
import jax
import jax.numpy as jnp
from jax import lax
from jax.sharding import PartitionSpec as P

D = 7168


def swiglu(rows, gate_w, up_w):
    gate_pre = jnp.dot(rows, gate_w, preferred_element_type=jnp.float32)
    up_pre = jnp.dot(rows, up_w, preferred_element_type=jnp.float32)
    return (jax.nn.silu(gate_pre) * up_pre).astype(jnp.bfloat16)


def shards(
    tokens,
    expert_ids,
    gate_q,
    importance,
    dense_gate,
    dense_up,
    dense_down,
    delta_gate,
    delta_up,
    delta_down,
    base_gate,
    base_up,
    base_down,
):
    groups = lax.axis_size("exp")
    splits = lax.axis_size("base")
    tok_rows, local_width = tokens.shape
    top_k = expert_ids.shape[1]
    local_experts = dense_gate.shape[0]
    capacity = tok_rows * top_k * 3 // (2 * local_experts * groups)
    dense_width = dense_gate.shape[2]
    low_width = delta_gate.shape[2]
    all_rows = tok_rows * groups
    slots = capacity * groups
    routing = lax.all_gather(
        jnp.concatenate([expert_ids, gate_q], axis=1), "exp", axis=0, tiled=True
    )
    own_rows = lax.all_gather(tokens, "base", axis=1, tiled=True)
    rows = lax.all_gather(own_rows, "exp", axis=0, tiled=True)
    ids, gates = (routing[:, :top_k], routing[:, top_k:])
    first = lax.axis_index("exp") * local_experts
    mine = first + jnp.arange(local_experts, dtype=jnp.int32)
    hit = ids[:, None, :] == mine[None, :, None]
    weight = jnp.sum(jnp.where(hit, gates[:, None, :].astype(jnp.float32), 0.0), axis=2) / 65536.0
    named = jnp.any(hit, axis=2)
    order = jnp.arange(all_rows, dtype=jnp.int32)
    block = order // tok_rows
    before = (block[:, None] == block[None, :]) & (order[None, :] < order[:, None])
    position = jnp.dot(
        before.astype(jnp.bfloat16), named.astype(jnp.bfloat16), preferred_element_type=jnp.float32
    ).astype(jnp.int32)
    slot = jnp.where(named, block[:, None] * capacity + position, -1)
    pick = jnp.arange(slots, dtype=jnp.int32)[None, :, None] == slot.T[:, None, :]
    select = pick.astype(jnp.bfloat16)
    shared = swiglu(own_rows, base_gate, base_up)
    partial_value = jnp.dot(shared, base_down, preferred_element_type=jnp.float32)
    base_own = lax.psum_scatter(
        partial_value.astype(jnp.bfloat16), "base", scatter_dimension=1, tiled=True
    )
    base_all = lax.all_gather(base_own, "exp", axis=0, tiled=True)
    packed = []
    for j in range(local_experts):
        hidden = swiglu(rows, dense_gate[j], dense_up[j])
        low = swiglu(rows, delta_gate[j], delta_up[j])
        both = jnp.concatenate([hidden, low], axis=1)
        packed.append(
            jnp.dot(select[j], both, preferred_element_type=jnp.float32).astype(jnp.bfloat16)
        )
    sent = jnp.stack(packed)
    full = lax.all_gather(sent, "base", axis=0, tiled=False)
    total = jnp.zeros((all_rows,), jnp.float32)
    for j in range(local_experts):
        hid = jnp.concatenate([full[b, j, :, :dense_width] for b in range(splits)], axis=1)
        low = jnp.concatenate([full[b, j, :, dense_width:] for b in range(splits)], axis=1)
        residual = jnp.dot(hid, dense_down[j], preferred_element_type=jnp.float32) - jnp.dot(
            low, delta_down[j], preferred_element_type=jnp.float32
        )
        residual = residual.astype(jnp.bfloat16).astype(jnp.float32)
        base_rows = jnp.dot(select[j], base_all, preferred_element_type=jnp.float32)
        deviation = residual - base_rows
        squares = jnp.sum(importance * deviation * deviation, axis=1)
        back = jnp.sum(jnp.where(pick[j], squares[:, None], 0.0), axis=0)
        total = total + weight[:, j] * back
    total = lax.psum(total / D, ("exp", "base"))
    return lax.dynamic_slice_in_dim(total, lax.axis_index("exp") * tok_rows, tok_rows)


def solution(mesh):
    in_specs = (
        P(("grp", "exp"), "base"),
        P(("grp", "exp"), None),
        P(("grp", "exp"), None),
        P("base"),
        P("exp", None, "base"),
        P("exp", None, "base"),
        P("exp", None, "base"),
        P("exp", None, "base"),
        P("exp", None, "base"),
        P("exp", None, "base"),
        P(None, "base"),
        P(None, "base"),
        P("base", None),
    )
    out_specs = P(("grp", "exp"))
    return jax.shard_map(shards, mesh=mesh, in_specs=in_specs, out_specs=out_specs, check_vma=False)
```

profile of v0, /device:TPU:0, one launch (start us, length us, event | category | flops | bytes accessed | tf_op | source)
XLA Modules:
  0.0 204.3 jit_solution(16887898204992520157)
XLA Ops:
  7.4 23.4 %all_gather.19 = bf16[64,7168]{1,0:T(8,128)(2,1)} all-gather(bf16[64,1792]{1,0:T(8,128)(2,1)} %param.13), channel_id=1, replica_groups=mesh['grp'=2,'exp'=4,'base'=4] {'base'}, dimensions={1}, use_global_device_ids=true | all-gather | bytes 1146880 | tf_op jit(solution)/shard_map/all_gather | solution.py:43
  30.9 3.1 %fusion.206 = f32[64,256]{1,0:T(8,128)S(1)} fusion(bf16[64,7168]{1,0:T(8,128)(2,1)} %all_gather.19, bf16[7168,256]{1,0:T(8,128)(2,1)} %param.23), kind=kOutput, calls=%fused_computation.267 | convolution fusion | flops 234881024 | bytes 4653056 | tf_op jit(solution)/shard_map/dot_general | solution.py:10
  34.0 6.8 %convolution_convert_fusion = bf16[64,7168]{1,0:T(8,128)(2,1)} fusion(bf16[256,7168]{1,0:T(8,128)(2,1)} %param.25, bf16[64,7168]{1,0:T(8,128)(2,1)S(1)} %copy-done.1, bf16[7168,256]{1,0:T(8,128)(2,1)} %param.24, f32[64,256]{1,0:T(8,128)S(1)} %fusion.206), kind=kOutput, calls=%fused_computation | convolution fusion | flops 470319104 | bytes 9240576 | tf_op jit(solution)/shard_map/dot_general | solution.py:61
  40.9 5.5 %all-gather.1 = s32[4,64,16]{1,2,0:T(8,128)S(1)} all-gather(s32[1,64,16]{1,2,0:T(8,128)S(1)} %add_bitcast_fusion), channel_id=1, replica_groups=mesh['grp'=2,'exp'=4,'base'=4] {'exp'}, dimensions={0}, use_global_device_ids=true | all-gather | bytes 20480 | tf_op jit(solution)/shard_map/all_gather | solution.py:40
  47.0 15.2 %all-gather.5.cloned.1.call-done = bf16[256,7168]{1,0:T(8,128)(2,1)} async-done(((bf16[64,7168]{1,0:T(8,128)(2,1)}), bf16[256,7168]{1,0:T(8,128)(2,1)}) %all-gather.5.cloned.1.call-update) | async-done | bytes 3670032 | tf_op jit(solution)/shard_map/all_gather | solution.py:44
  62.2 3.4 %fusion.88 = f32[256,32]{0,1:T(8,128)S(1)} fusion(bf16[256,7168]{1,0:T(8,128)(2,1)} %all-gather.5.cloned.1.call-done, bf16[4,7168,32]{1,2,0:T(8,128)(2,1)S(1)} %copy-done.2), kind=kOutput, calls=%fused_computation.97 | convolution fusion | flops 117440512 | bytes 4161536 | tf_op jit(solution)/shard_map/dot_general | solution.py:10
  65.6 3.8 %fusion.10 = f32[256,256]{0,1:T(8,128)S(1)} fusion(bf16[256,7168]{1,0:T(8,128)(2,1)S(1)} %copy-done, bf16[4,7168,256]{2,1,0:T(8,128)(2,1)} %param.17), kind=kOutput, calls=%fused_computation.11 | convolution fusion | flops 939524096 | bytes 7602176 | tf_op jit(solution)/shard_map/dot_general | solution.py:10
  69.5 1.2 fusion.80
  70.7 3.9 %fusion.60 = bf16[256,256]{0,1:T(8,128)(2,1)S(1)} fusion(bf16[256,7168]{1,0:T(8,128)(2,1)S(1)} %copy-done, bf16[4,7168,256]{2,1,0:T(8,128)(2,1)} %param.18, f32[256,256]{0,1:T(8,128)S(1)} %fusion.10), kind=kOutput, calls=%fused_computation.69 | convolution fusion | flops 939917312 | bytes 7733248 | tf_op jit(solution)/shard_map/dot_general | solution.py:11
  74.8 1.2 fusion.91
  76.0 1.2 fusion.94
  77.2 1.2 fusion.97
  78.5 1.6 fusion.14
  80.1 1.6 fusion.18
  81.7 1.2 fusion.79
  82.9 1.2 fusion.78
  84.2 3.9 %fusion.63 = bf16[256,256]{0,1:T(8,128)(2,1)S(1)} fusion(bf16[256,7168]{1,0:T(8,128)(2,1)S(1)} %copy-done, bf16[4,7168,256]{2,1,0:T(8,128)(2,1)} %param.18, f32[256,256]{0,1:T(8,128)S(1)} %fusion.14), kind=kOutput, calls=%fused_computation.70 | convolution fusion | flops 939917312 | bytes 7733248 | tf_op jit(solution)/shard_map/dot_general | solution.py:11
  88.1 3.7 %fusion.66 = bf16[256,256]{0,1:T(8,128)(2,1)S(1)} fusion(bf16[256,7168]{1,0:T(8,128)(2,1)S(1)} %copy-done, bf16[4,7168,256]{2,1,0:T(8,128)(2,1)} %param.18, f32[256,256]{0,1:T(8,128)S(1)} %fusion.18), kind=kOutput, calls=%fused_computation.71 | convolution fusion | flops 939917312 | bytes 7733248 | tf_op jit(solution)/shard_map/dot_general | solution.py:11
  92.3 1.2 fusion.77
  93.5 1.6 fusion.22
  95.1 3.7 %fusion.69 = bf16[256,256]{0,1:T(8,128)(2,1)S(1)} fusion(bf16[256,7168]{1,0:T(8,128)(2,1)S(1)} %copy-done, bf16[4,7168,256]{2,1,0:T(8,128)(2,1)} %param.18, f32[256,256]{0,1:T(8,128)S(1)} %fusion.22), kind=kOutput, calls=%fused_computation.72 | convolution fusion | flops 939917312 | bytes 7733248 | tf_op jit(solution)/shard_map/dot_general | solution.py:11
  99.1 0.9 pad_maximum_fusion
  100.2 9.8 %all_gather.23 = bf16[256,1792]{1,0:T(8,128)(2,1)S(1)} all-gather(bf16[64,1792]{1,0:T(8,128)(2,1)} %reduce-scatter.2.cloned.1.call-done), channel_id=1, replica_groups=mesh['grp'=2,'exp'=4,'base'=4] {'exp'}, dimensions={0}, use_global_device_ids=true | all-gather | bytes 1146880 | tf_op jit(solution)/shard_map/all_gather | solution.py:65
  110.0 40.2 %all-gather.7.cloned.1.call-done = bf16[16,192,288]{2,1,0:T(8,128)(2,1)} async-done(((bf16[4,192,288]{2,1,0:T(8,128)(2,1)}), bf16[16,192,288]{2,1,0:T(8,128)(2,1)}) %all-gather.7.cloned.1.call-update) | async-done | bytes 1769488 | tf_op jit(solution)/shard_map/all_gather | solution.py:75
  150.2 1.2 slice_bitcast_fusion.39
  151.4 1.7 slice_bitcast_fusion.23
  153.1 3.1 %fusion.4 = f32[192,1792]{1,0:T(8,128)S(1)} fusion(bf16[4,1024,1792]{2,1,0:T(8,128)(2,1)} %param.19, bf16[192,256]{1,0:T(8,128)(2,1)S(1)} %get-tuple-element.34, bf16[192,256]{1,0:T(8,128)(2,1)S(1)} %get-tuple-element.35, bf16[192,256]{1,0:T(8,128)(2,1)S(1)} %get-tuple-element.36, bf16[192,256]{1,0:T(8,128)(2,1)S(1)} %get-tuple-element.25), kind=kOutput, calls=%fused_computation.5 | convolution fusion | flops 706215936 | bytes 5439488 | tf_op jit(solution)/shard_map/dot_general | solution.py:80
  157.1 3.1 %fusion = f32[192,1792]{1,0:T(8,128)S(1)} fusion(bf16[4,1024,1792]{2,1,0:T(8,128)(2,1)} %param.19, bf16[192,256]{1,0:T(8,128)(2,1)S(1)} %get-tuple-element.26, bf16[192,256]{1,0:T(8,128)(2,1)S(1)} %get-tuple-element.27, bf16[192,256]{1,0:T(8,128)(2,1)S(1)} %get-tuple-element.28, bf16[192,256]{1,0:T(8,128)(2,1)S(1)} %get-tuple-element.29), kind=kOutput, calls=%fused_computation.1 | convolution fusion | flops 706215936 | bytes 5439488 | tf_op jit(solution)/shard_map/dot_general | solution.py:80
  161.2 0.9 fusion.2
  163.0 0.9 fusion.6
  165.0 31.3 %psum.7 = f32[256]{0:T(256)S(1)} all-reduce(f32[256]{0:T(256)S(1)} %add_multiply_fusion), channel_id=1, replica_groups=mesh['grp'=2,'exp'=4,'base'=4] {'exp','base'}, use_global_device_ids=true, to_apply=%region_11.12 | all-reduce | flops 256 | bytes 2048 | tf_op jit(solution)/shard_map/psum | solution.py:89
  196.3 0.6 dynamic_slice.3
  (67 shorter events, 5.6 us)
Async XLA Ops:
  7.4 54.8 %all-gather.5.cloned.1.call-start = ((), (), s32[]{:S(2)}) async-start(), calls=%async_computation.1 | async-start | bytes 4587520 | tf_op jit(solution)/shard_map/all_gather | solution.py:44
  30.8 3.2 %copy-start.1 = (bf16[64,7168]{1,0:T(8,128)(2,1)S(1)}, bf16[64,7168]{1,0:T(8,128)(2,1)}, u32[]{:S(2)}) copy-start(bf16[64,7168]{1,0:T(8,128)(2,1)} %all_gather.19) | copy-start | bytes 2752516
  30.8 69.4 %reduce-scatter.2.cloned.1.call-start = ((), (), s32[]{:S(2)}) async-start(), calls=%async_computation.2 | async-start | bytes 1146880 | tf_op jit(solution)/shard_map/reduce_scatter | solution.py:62
  34.0 6.9 %copy-start.6 = (s32[64,8]{0,1:T(8,128)S(1)}, s32[64,8]{0,1:T(8,128)}, u32[]{:S(2)}) copy-start(s32[64,8]{0,1:T(8,128)} %param.15) | copy-start | bytes 6148
  34.0 6.9 %copy-start.7 = (s32[64,8]{0,1:T(8,128)S(1)}, s32[64,8]{0,1:T(8,128)}, u32[]{:S(2)}) copy-start(s32[64,8]{0,1:T(8,128)} %param.14) | copy-start | bytes 6148
  34.0 28.2 %copy-start.2 = (bf16[4,7168,32]{1,2,0:T(8,128)(2,1)S(1)}, bf16[4,7168,32]{1,2,0:T(8,128)(2,1)}, u32[]{:S(2)}) copy-start(bf16[4,7168,32]{1,2,0:T(8,128)(2,1)} %param.20) | copy-start | bytes 5505028
  40.8 109.4 %all-gather.7.cloned.1.call-start = ((), (), s32[]{:S(2)}) async-start(), calls=%async_computation.3 | async-start | bytes 2949120 | tf_op jit(solution)/shard_map/all_gather | solution.py:75
  62.2 3.4 %copy-start = (bf16[256,7168]{1,0:T(8,128)(2,1)S(1)}, bf16[256,7168]{1,0:T(8,128)(2,1)}, u32[]{:S(2)}) copy-start(bf16[256,7168]{1,0:T(8,128)(2,1)} %all-gather.5.cloned.1.call-done) | copy-start | bytes 11010052
  65.6 3.8 %copy-start.3 = (bf16[4,7168,32]{1,2,0:T(8,128)(2,1)S(1)}, bf16[4,7168,32]{1,2,0:T(8,128)(2,1)}, u32[]{:S(2)}) copy-start(bf16[4,7168,32]{1,2,0:T(8,128)(2,1)} %param.21) | copy-start | bytes 5505028
  69.5 9.0 %slice-start = ((s8[14680064]{0:T(1024)(128)(4,1)}), s8[4194304]{0:T(1024)(128)(4,1)S(1)}, s32[]{:S(2)}) async-start(s8[14680064]{0:T(1024)(128)(4,1)} %bitcast.227), calls=%async_computation.4 | async-start | bytes 8388608
  70.7 7.8 %slice-start.1 = ((s8[14680064]{0:T(1024)(128)(4,1)}), s8[4194304]{0:T(1024)(128)(4,1)S(1)}, s32[]{:S(2)}) async-start(s8[14680064]{0:T(1024)(128)(4,1)} %bitcast.227), calls=%async_computation.5 | async-start | bytes 8388608
  70.7 7.8 %slice-start.2 = ((s8[14680064]{0:T(1024)(128)(4,1)}), s8[4194304]{0:T(1024)(128)(4,1)S(1)}, s32[]{:S(2)}) async-start(s8[14680064]{0:T(1024)(128)(4,1)} %bitcast.227), calls=%async_computation.6 | async-start | bytes 8388608
  76.0 2.5 %slice-start.3 = ((s8[14680064]{0:T(1024)(128)(4,1)}), s8[2097152]{0:T(1024)(128)(4,1)S(1)}, s32[]{:S(2)}) async-start(s8[14680064]{0:T(1024)(128)(4,1)} %bitcast.227), calls=%async_computation.7 | async-start | bytes 4194304
  151.4 9.8 %slice-start.4 = ((s8[14680064]{0:T(1024)(128)(4,1)}), s8[2097152]{0:T(1024)(128)(4,1)S(1)}, s32[]{:S(2)}) async-start(s8[14680064]{0:T(1024)(128)(4,1)} %bitcast.229), calls=%async_computation.8 | async-start | bytes 4194304
  153.1 3.1 %copy-start.4 = (bf16[4,128,1792]{2,1,0:T(8,128)(2,1)S(1)}, bf16[4,128,1792]{2,1,0:T(8,128)(2,1)}, u32[]{:S(2)}) copy-start(bf16[4,128,1792]{2,1,0:T(8,128)(2,1)} %param.22) | copy-start | bytes 5505028
  153.1 3.5 %copy-start.5 = (f32[1792]{0:T(1024)S(1)}, f32[1792]{0:T(1024)}, u32[]{:S(2)}) copy-start(f32[1792]{0:T(1024)} %param.16) | copy-start | bytes 21508
  153.1 8.0 %slice-start.5 = ((s8[14680064]{0:T(1024)(128)(4,1)}), s8[4194304]{0:T(1024)(128)(4,1)S(1)}, s32[]{:S(2)}) async-start(s8[14680064]{0:T(1024)(128)(4,1)} %bitcast.229), calls=%async_computation.9 | async-start | bytes 8388608
  156.6 4.5 %slice-start.6 = ((s8[14680064]{0:T(1024)(128)(4,1)}), s8[4194304]{0:T(1024)(128)(4,1)S(1)}, s32[]{:S(2)}) async-start(s8[14680064]{0:T(1024)(128)(4,1)} %bitcast.229), calls=%async_computation.10 | async-start | bytes 8388608
  157.1 4.1 %slice-start.7 = ((s8[14680064]{0:T(1024)(128)(4,1)}), s8[4194304]{0:T(1024)(128)(4,1)S(1)}, s32[]{:S(2)}) async-start(s8[14680064]{0:T(1024)(128)(4,1)} %bitcast.229), calls=%async_computation.11 | async-start | bytes 8388608
Sparse Core Ops, SparseCore 0:
  30.9 31.2 all-gather.4
Sparse Core Ops, SparseCore 1:
  40.9 24.4 reduce-scatter.1
  100.1 50.0 all-gather.6
where the time goes:
time: 205 us; the launch traced here: 204 us
  blocking collectives  70 us (34%)
  matrix products  58.1 us (28%)
  waiting for transfers between devices  55.4 us (27%)
  between operations  15.3 us (7%)
  local copies, waits for them, and re-layouts  3.8 us (2%)
    all_gather x1, waiting for transfers between devices, shards(): full = lax.all_gather(sent, 'base', axis=0, tiled=False)  40.2 us
    psum x1, blocking collectives, shards(): total = lax.psum(total / D, ('exp', 'base'))  31.3 us
    all_gather x1, blocking collectives, shards(): own_rows = lax.all_gather(tokens, 'base', axis=1, tiled=True)  23.4 us
    dot_general x8, matrix products, swiglu(): up_pre = jnp.dot(rows, up_w, preferred_element_type=jnp.float32)  20.1 us
    dot_general x9, matrix products, swiglu(): gate_pre = jnp.dot(rows, gate_w, preferred_element_type=jnp.float32)  18.7 us
    all_gather x1, waiting for transfers between devices, shards(): rows = lax.all_gather(own_rows, 'exp', axis=0, tiled=True)  15.2 us
    all_gather x1, blocking collectives, shards(): base_all = lax.all_gather(base_own, 'exp', axis=0, tiled=True)  9.8 us
    dot_general x4, matrix products, shards(): jnp.dot(hid, dense_down[j], preferred_element_type=jnp.float32)  7.97 us
  transfers between devices with their start and end apart: 3, of which 2 were waited for; matrix products, arithmetic and copies ran while one was open for 24% of the time, Pallas kernels for 0%

commit v1 on v0

--- a/solution.py
+++ b/solution.py
@@ -41,7 +41,6 @@
         jnp.concatenate([expert_ids, gate_q], axis=1), "exp", axis=0, tiled=True
     )
     own_rows = lax.all_gather(tokens, "base", axis=1, tiled=True)
-    rows = lax.all_gather(own_rows, "exp", axis=0, tiled=True)
     ids, gates = (routing[:, :top_k], routing[:, top_k:])
     first = lax.axis_index("exp") * local_experts
     mine = first + jnp.arange(local_experts, dtype=jnp.int32)
@@ -62,7 +61,11 @@
     base_own = lax.psum_scatter(
         partial_value.astype(jnp.bfloat16), "base", scatter_dimension=1, tiled=True
     )
-    base_all = lax.all_gather(base_own, "exp", axis=0, tiled=True)
+    rows, base_all = jnp.split(
+        lax.all_gather(jnp.concatenate([own_rows, base_own], axis=1), "exp", axis=0, tiled=True),
+        [own_rows.shape[1]],
+        axis=1,
+    )
     packed = []
     for j in range(local_experts):
         hidden = swiglu(rows, dense_gate[j], dense_up[j])

time: 205 us -> 271 us (1.32)
  waiting for transfers between devices: 55.4 us -> 105 us
  matrix products: 58.1 us -> 84.4 us
  blocking collectives: 70 us -> 59.7 us
    reduce_scatter x1, waiting for transfers between devices: 0.03 us -> 24.8 us  [shards(): lax.psum_scatter(partial_value.astype(jnp.bfloat16), 'base', scatter_dime...]
    all_gather x1, waiting for transfers between devices: 15.2 us -> 29.8 us  [shards(): lax.all_gather(jnp.concatenate([own_rows, base_own], axis=1), 'exp', axis...]
    dot_general x9, matrix products: 18.7 us -> 32.5 us  [swiglu(): gate_pre = jnp.dot(rows, gate_w, preferred_element_type=jnp.float32)]
    all_gather x1, waiting for transfers between devices: 40.2 us -> 50.5 us  [shards(): full = lax.all_gather(sent, 'base', axis=0, tiled=False)]
    all_gather x1 -> x0, blocking collectives: 9.8 us -> none  [shards(): base_all = lax.all_gather(base_own, 'exp', axis=0, tiled=True)]
    dot_general x8, matrix products: 20.1 us -> 29 us  [swiglu(): up_pre = jnp.dot(rows, up_w, preferred_element_type=jnp.float32)]
    dot_general x4, matrix products: 7.97 us -> 11.9 us  [shards(): jnp.dot(hid, dense_down[j], preferred_element_type=jnp.float32)]
  transfers between devices with their start and end apart: 3 -> 3, of which waited for: 2 -> 3; matrix products, arithmetic and copies ran while one was open for 24% -> 0% of each run, Pallas kernels for 0% -> 0%
where the time goes in v1:
time: 271 us; the launch traced here: 270 us
  waiting for transfers between devices  105 us (39%)
  matrix products  84.4 us (31%)
  blocking collectives  59.7 us (22%)
  between operations  13.5 us (5%)
  local copies, waits for them, and re-layouts  4.05 us (1%)
  other arithmetic  3.55 us (1%)
    all_gather x1, waiting for transfers between devices, shards(): full = lax.all_gather(sent, 'base', axis=0, tiled=False)  50.5 us
    dot_general x9, matrix products, swiglu(): gate_pre = jnp.dot(rows, gate_w, preferred_element_type=jnp.float32)  32.5 us
    psum x1, blocking collectives, shards(): total = lax.psum(total / D, ('exp', 'base'))  31.3 us
    all_gather x1, waiting for transfers between devices, shards(): lax.all_gather(jnp.concatenate([own_rows, base_own], axis=1), 'exp', axis...  29.8 us
    dot_general x8, matrix products, swiglu(): up_pre = jnp.dot(rows, up_w, preferred_element_type=jnp.float32)  29 us
    reduce_scatter x1, waiting for transfers between devices, shards(): lax.psum_scatter(partial_value.astype(jnp.bfloat16), 'base', scatter_dime...  24.8 us
    all_gather x1, blocking collectives, shards(): own_rows = lax.all_gather(tokens, 'base', axis=1, tiled=True)  23 us
    dot_general x4, matrix products, shards(): jnp.dot(hid, dense_down[j], preferred_element_type=jnp.float32)  11.9 us
  transfers between devices with their start and end apart: 3, of which 3 were waited for; matrix products, arithmetic and copies ran while one was open for 0% of the time, Pallas kernels for 0%

profile of v1, /device:TPU:0, one launch (start us, length us, event | category | flops | bytes accessed | tf_op | source)
XLA Modules:
  0.0 270.4 jit_solution(386038696704940868)
XLA Ops:
  6.5 23.0 %all_gather.16 = bf16[64,7168]{1,0:T(8,128)(2,1)S(1)} all-gather(bf16[64,1792]{1,0:T(8,128)(2,1)} %param.13), channel_id=1, replica_groups=mesh['grp'=2,'exp'=4,'base'=4] {'base'}, dimensions={1}, use_global_device_ids=true | all-gather | bytes 1146880 | tf_op jit(solution)/shard_map/all_gather | solution.py:43
  29.5 2.7 %fusion.226 = f32[64,256]{1,0:T(8,128)S(1)} fusion(bf16[64,7168]{1,0:T(8,128)(2,1)S(1)} %all_gather.16, bf16[7168,256]{1,0:T(8,128)(2,1)} %param.23), kind=kOutput, calls=%fused_computation.288 | convolution fusion | flops 234881024 | bytes 4653056 | tf_op jit(solution)/shard_map/dot_general | solution.py:10
  32.2 6.4 %convolution_convert_fusion = bf16[64,7168]{1,0:T(8,128)(2,1)} fusion(bf16[256,7168]{1,0:T(8,128)(2,1)} %param.25, bf16[64,7168]{1,0:T(8,128)(2,1)S(1)} %all_gather.16, bf16[7168,256]{1,0:T(8,128)(2,1)} %param.24, f32[64,256]{1,0:T(8,128)S(1)} %fusion.226), kind=kOutput, calls=%fused_computation | convolution fusion | flops 470319104 | bytes 9240576 | tf_op jit(solution)/shard_map/dot_general | solution.py:60
  38.7 24.8 %reduce-scatter.2.cloned.1.call-done = bf16[64,1792]{1,0:T(8,128)(2,1)} async-done(((bf16[64,7168]{1,0:T(8,128)(2,1)}), bf16[64,1792]{1,0:T(8,128)(2,1)}) %reduce-scatter.2.cloned.1.call-update) | async-done | bytes 229392 | tf_op jit(solution)/shard_map/reduce_scatter | solution.py:61
  63.5 2.1 pad_maximum_fusion
  65.6 5.4 %all-gather.1 = s32[4,64,16]{1,2,0:T(8,128)S(1)} all-gather(s32[1,64,16]{1,2,0:T(8,128)S(1)} %add_bitcast_fusion), channel_id=1, replica_groups=mesh['grp'=2,'exp'=4,'base'=4] {'exp'}, dimensions={0}, use_global_device_ids=true | all-gather | bytes 20480 | tf_op jit(solution)/shard_map/all_gather | solution.py:40
  71.6 29.8 %all-gather.5.cloned.1.call-done = bf16[256,8960]{1,0:T(8,128)(2,1)} async-done(((bf16[64,8960]{1,0:T(8,128)(2,1)}), bf16[256,8960]{1,0:T(8,128)(2,1)}) %all-gather.5.cloned.1.call-update) | async-done | bytes 4587536 | tf_op jit(solution)/shard_map/all_gather | solution.py:65
  101.4 3.4 %fusion.98 = f32[256,32]{0,1:T(8,128)S(1)} fusion(bf16[4,7168,32]{1,2,0:T(8,128)(2,1)S(1)} %copy-done.4, bf16[256,8960]{1,0:T(8,128)(2,1)} %all-gather.5.cloned.1.call-done), kind=kOutput, calls=%fused_computation.108 | convolution fusion | flops 117440512 | bytes 4161536 | tf_op jit(solution)/shard_map/dot_general | solution.py:10
  104.8 5.5 %fusion.18 = f32[256,256]{0,1:T(8,128)S(1)} fusion(bf16[4,7168,256]{2,1,0:T(8,128)(2,1)} %param.17, bf16[256,8960]{1,0:T(8,128)(2,1)} %all-gather.5.cloned.1.call-done), kind=kOutput, calls=%fused_computation.19 | convolution fusion | flops 939524096 | bytes 7602176 | tf_op jit(solution)/shard_map/dot_general | solution.py:10
  110.3 4.1 %fusion.78 = bf16[256,32]{0,1:T(8,128)(2,1)S(1)} fusion(bf16[4,7168,32]{1,2,0:T(8,128)(2,1)} %param.21, f32[256,32]{0,1:T(8,128)S(1)} %fusion.98, bf16[256,8960]{1,0:T(8,128)(2,1)} %all-gather.5.cloned.1.call-done), kind=kOutput, calls=%fused_computation.85 | convolution fusion | flops 117489664 | bytes 4177920 | tf_op jit(solution)/shard_map/dot_general | solution.py:11
  114.4 3.9 %fusion.66 = bf16[256,256]{0,1:T(8,128)(2,1)S(1)} fusion(bf16[4,7168,256]{2,1,0:T(8,128)(2,1)S(1)} %copy-done.3, f32[256,256]{0,1:T(8,128)S(1)} %fusion.18, bf16[256,8960]{1,0:T(8,128)(2,1)} %all-gather.5.cloned.1.call-done), kind=kOutput, calls=%fused_computation.71 | convolution fusion | flops 939917312 | bytes 7733248 | tf_op jit(solution)/shard_map/dot_general | solution.py:11
  118.5 3.2 %fusion.95 = f32[256,32]{0,1:T(8,128)S(1)} fusion(bf16[4,7168,32]{1,2,0:T(8,128)(2,1)S(1)} %copy-done.4, bf16[256,8960]{1,0:T(8,128)(2,1)} %all-gather.5.cloned.1.call-done), kind=kOutput, calls=%fused_computation.105 | convolution fusion | flops 117440512 | bytes 4161536 | tf_op jit(solution)/shard_map/dot_general | solution.py:10
  121.8 3.7 %fusion.14 = f32[256,256]{0,1:T(8,128)S(1)} fusion(bf16[4,7168,256]{2,1,0:T(8,128)(2,1)S(1)} %bitcast.208, bf16[256,8960]{1,0:T(8,128)(2,1)} %all-gather.5.cloned.1.call-done), kind=kOutput, calls=%fused_computation.15 | convolution fusion | flops 939524096 | bytes 7602176 | tf_op jit(solution)/shard_map/dot_general | solution.py:10
  125.4 3.3 %fusion.79 = bf16[256,32]{0,1:T(8,128)(2,1)S(1)} fusion(bf16[4,7168,32]{1,2,0:T(8,128)(2,1)} %param.21, f32[256,32]{0,1:T(8,128)S(1)} %fusion.95, bf16[256,8960]{1,0:T(8,128)(2,1)} %all-gather.5.cloned.1.call-done), kind=kOutput, calls=%fused_computation.86 | convolution fusion | flops 117489664 | bytes 4177920 | tf_op jit(solution)/shard_map/dot_general | solution.py:11
  128.8 3.7 %fusion.63 = bf16[256,256]{0,1:T(8,128)(2,1)S(1)} fusion(bf16[4,7168,256]{2,1,0:T(8,128)(2,1)S(1)} %copy-done.3, f32[256,256]{0,1:T(8,128)S(1)} %fusion.14, bf16[256,8960]{1,0:T(8,128)(2,1)} %all-gather.5.cloned.1.call-done), kind=kOutput, calls=%fused_computation.70 | convolution fusion | flops 939917312 | bytes 7733248 | tf_op jit(solution)/shard_map/dot_general | solution.py:11
  132.7 3.2 %fusion.92 = f32[256,32]{0,1:T(8,128)S(1)} fusion(bf16[4,7168,32]{1,2,0:T(8,128)(2,1)S(1)} %copy-done.4, bf16[256,8960]{1,0:T(8,128)(2,1)} %all-gather.5.cloned.1.call-done), kind=kOutput, calls=%fused_computation.102 | convolution fusion | flops 117440512 | bytes 4161536 | tf_op jit(solution)/shard_map/dot_general | solution.py:10
  135.9 3.9 %fusion.10 = f32[256,256]{0,1:T(8,128)S(1)} fusion(bf16[4,7168,256]{2,1,0:T(8,128)(2,1)S(1)} %bitcast.208, bf16[256,8960]{1,0:T(8,128)(2,1)} %all-gather.5.cloned.1.call-done), kind=kOutput, calls=%fused_computation.11 | convolution fusion | flops 939524096 | bytes 7602176 | tf_op jit(solution)/shard_map/dot_general | solution.py:10
  139.8 3.3 %fusion.80 = bf16[256,32]{0,1:T(8,128)(2,1)S(1)} fusion(bf16[4,7168,32]{1,2,0:T(8,128)(2,1)} %param.21, f32[256,32]{0,1:T(8,128)S(1)} %fusion.92, bf16[256,8960]{1,0:T(8,128)(2,1)} %all-gather.5.cloned.1.call-done), kind=kOutput, calls=%fused_computation.87 | convolution fusion | flops 117489664 | bytes 4177920 | tf_op jit(solution)/shard_map/dot_general | solution.py:11
  143.2 3.7 %fusion.60 = bf16[256,256]{0,1:T(8,128)(2,1)S(1)} fusion(bf16[4,7168,256]{2,1,0:T(8,128)(2,1)S(1)} %copy-done.3, f32[256,256]{0,1:T(8,128)S(1)} %fusion.10, bf16[256,8960]{1,0:T(8,128)(2,1)} %all-gather.5.cloned.1.call-done), kind=kOutput, calls=%fused_computation.69 | convolution fusion | flops 939917312 | bytes 7733248 | tf_op jit(solution)/shard_map/dot_general | solution.py:11
  147.1 3.2 %fusion.101 = f32[256,32]{0,1:T(8,128)S(1)} fusion(bf16[4,7168,32]{1,2,0:T(8,128)(2,1)S(1)} %copy-done.4, bf16[256,8960]{1,0:T(8,128)(2,1)} %all-gather.5.cloned.1.call-done), kind=kOutput, calls=%fused_computation.111 | convolution fusion | flops 117440512 | bytes 4161536 | tf_op jit(solution)/shard_map/dot_general | solution.py:10
  150.4 3.7 %fusion.22 = f32[256,256]{0,1:T(8,128)S(1)} fusion(bf16[4,7168,256]{2,1,0:T(8,128)(2,1)S(1)} %bitcast.208, bf16[256,8960]{1,0:T(8,128)(2,1)} %all-gather.5.cloned.1.call-done), kind=kOutput, calls=%fused_computation.23 | convolution fusion | flops 939524096 | bytes 7602176 | tf_op jit(solution)/shard_map/dot_general | solution.py:10
  154.0 3.3 %fusion.77 = bf16[256,32]{0,1:T(8,128)(2,1)S(1)} fusion(bf16[4,7168,32]{1,2,0:T(8,128)(2,1)} %param.21, f32[256,32]{0,1:T(8,128)S(1)} %fusion.101, bf16[256,8960]{1,0:T(8,128)(2,1)} %all-gather.5.cloned.1.call-done), kind=kOutput, calls=%fused_computation.84 | convolution fusion | flops 117489664 | bytes 4177920 | tf_op jit(solution)/shard_map/dot_general | solution.py:11
  157.4 3.7 %fusion.69 = bf16[256,256]{0,1:T(8,128)(2,1)S(1)} fusion(bf16[4,7168,256]{2,1,0:T(8,128)(2,1)S(1)} %copy-done.3, f32[256,256]{0,1:T(8,128)S(1)} %fusion.22, bf16[256,8960]{1,0:T(8,128)(2,1)} %all-gather.5.cloned.1.call-done), kind=kOutput, calls=%fused_computation.72 | convolution fusion | flops 939917312 | bytes 7733248 | tf_op jit(solution)/shard_map/dot_general | solution.py:11
  161.3 1.0 pad_maximum_fusion.1
  162.4 50.5 %all-gather.7.cloned.1.call-done = bf16[16,192,288]{2,1,0:T(8,128)(2,1)} async-done(((bf16[4,192,288]{2,1,0:T(8,128)(2,1)}), bf16[16,192,288]{2,1,0:T(8,128)(2,1)}) %all-gather.7.cloned.1.call-update) | async-done | bytes 1769488 | tf_op jit(solution)/shard_map/all_gather | solution.py:78
  213.0 1.2 slice_bitcast_fusion.39
  214.1 1.6 slice_bitcast_fusion.23
  215.7 2.9 %fusion.4 = f32[192,1792]{1,0:T(8,128)S(1)} fusion(bf16[4,1024,1792]{2,1,0:T(8,128)(2,1)} %param.19, bf16[192,256]{1,0:T(8,128)(2,1)S(1)} %get-tuple-element.34, bf16[192,256]{1,0:T(8,128)(2,1)S(1)} %get-tuple-element.35, bf16[192,256]{1,0:T(8,128)(2,1)S(1)} %get-tuple-element.36, bf16[192,256]{1,0:T(8,128)(2,1)S(1)} %get-tuple-element.25), kind=kOutput, calls=%fused_computation.5 | convolution fusion | flops 706215936 | bytes 5439488 | tf_op jit(solution)/shard_map/dot_general | solution.py:83
  218.6 2.9 %fusion = f32[192,1792]{1,0:T(8,128)S(1)} fusion(bf16[4,1024,1792]{2,1,0:T(8,128)(2,1)} %param.19, bf16[192,256]{1,0:T(8,128)(2,1)S(1)} %get-tuple-element.26, bf16[192,256]{1,0:T(8,128)(2,1)S(1)} %get-tuple-element.27, bf16[192,256]{1,0:T(8,128)(2,1)S(1)} %get-tuple-element.28, bf16[192,256]{1,0:T(8,128)(2,1)S(1)} %get-tuple-element.29), kind=kOutput, calls=%fused_computation.1 | convolution fusion | flops 706215936 | bytes 5439488 | tf_op jit(solution)/shard_map/dot_general | solution.py:83
  221.6 2.9 %fusion.2 = f32[192,1792]{1,0:T(8,128)S(1)} fusion(bf16[4,1024,1792]{2,1,0:T(8,128)(2,1)} %param.19, bf16[192,256]{1,0:T(8,128)(2,1)S(1)} %get-tuple-element.30, bf16[192,256]{1,0:T(8,128)(2,1)S(1)} %get-tuple-element.31, bf16[192,256]{1,0:T(8,128)(2,1)S(1)} %get-tuple-element.32, bf16[192,256]{1,0:T(8,128)(2,1)S(1)} %get-tuple-element.33), kind=kOutput, calls=%fused_computation.3 | convolution fusion | flops 706215936 | bytes 5439488 | tf_op jit(solution)/shard_map/dot_general | solution.py:83
  224.6 3.1 %fusion.6 = f32[192,1792]{1,0:T(8,128)S(1)} fusion(bf16[4,1024,1792]{2,1,0:T(8,128)(2,1)} %param.19, bf16[192,256]{1,0:T(8,128)(2,1)S(1)} %get-tuple-element.37, bf16[192,256]{1,0:T(8,128)(2,1)S(1)} %get-tuple-element.38, bf16[192,256]{1,0:T(8,128)(2,1)S(1)} %get-tuple-element.39, bf16[192,256]{1,0:T(8,128)(2,1)S(1)} %get-tuple-element.40), kind=kOutput, calls=%fused_computation.7 | convolution fusion | flops 706215936 | bytes 5439488 | tf_op jit(solution)/shard_map/dot_general | solution.py:83
  231.9 31.3 %psum.7 = f32[256]{0:T(256)S(1)} all-reduce(f32[256]{0:T(256)S(1)} %add_multiply_fusion), channel_id=1, replica_groups=mesh['grp'=2,'exp'=4,'base'=4] {'exp','base'}, use_global_device_ids=true, to_apply=%region_11.12 | all-reduce | flops 256 | bytes 2048 | tf_op jit(solution)/shard_map/psum | solution.py:92
  (59 shorter events, 6.6 us)
Async XLA Ops:
  6.5 56.9 %reduce-scatter.2.cloned.1.call-start = ((), (), s32[]{:S(2)}) async-start(), calls=%async_computation.1 | async-start | bytes 1146880 | tf_op jit(solution)/shard_map/reduce_scatter | solution.py:61
  38.6 27.0 %copy-start.1 = (s32[64,8]{0,1:T(8,128)S(1)}, s32[64,8]{0,1:T(8,128)}, u32[]{:S(2)}) copy-start(s32[64,8]{0,1:T(8,128)} %param.15) | copy-start | bytes 6148
  38.6 27.0 %copy-start.2 = (s32[64,8]{0,1:T(8,128)S(1)}, s32[64,8]{0,1:T(8,128)}, u32[]{:S(2)}) copy-start(s32[64,8]{0,1:T(8,128)} %param.14) | copy-start | bytes 6148
  38.6 62.7 %copy-start.4 = (bf16[4,7168,32]{1,2,0:T(8,128)(2,1)S(1)}, bf16[4,7168,32]{1,2,0:T(8,128)(2,1)}, u32[]{:S(2)}) copy-start(bf16[4,7168,32]{1,2,0:T(8,128)(2,1)} %param.20) | copy-start | bytes 5505028
  38.7 62.7 %all-gather.5.cloned.1.call-start = ((), (), s32[]{:S(2)}) async-start(), calls=%async_computation.2 | async-start | bytes 5734400 | tf_op jit(solution)/shard_map/all_gather | solution.py:65
  65.6 147.4 %all-gather.7.cloned.1.call-start = ((), (), s32[]{:S(2)}) async-start(), calls=%async_computation.3 | async-start | bytes 2949120 | tf_op jit(solution)/shard_map/all_gather | solution.py:78
  101.4 13.0 %copy-start.3 = (bf16[4,7168,256]{2,1,0:T(8,128)(2,1)S(1)}, bf16[4,7168,256]{2,1,0:T(8,128)(2,1)}, u32[]{:S(2)}) copy-start(bf16[4,7168,256]{2,1,0:T(8,128)(2,1)} %param.18) | copy-start | bytes 44040196
  104.7 17.0 %slice-start = ((s8[14680064]{0:T(1024)(128)(4,1)}), s8[4194304]{0:T(1024)(128)(4,1)S(1)}, s32[]{:S(2)}) async-start(s8[14680064]{0:T(1024)(128)(4,1)} %bitcast.207), calls=%async_computation.4 | async-start | bytes 8388608
  104.8 16.9 %slice-start.1 = ((s8[14680064]{0:T(1024)(128)(4,1)}), s8[4194304]{0:T(1024)(128)(4,1)S(1)}, s32[]{:S(2)}) async-start(s8[14680064]{0:T(1024)(128)(4,1)} %bitcast.207), calls=%async_computation.5 | async-start | bytes 8388608
  114.3 7.4 %slice-start.2 = ((s8[14680064]{0:T(1024)(128)(4,1)}), s8[4194304]{0:T(1024)(128)(4,1)S(1)}, s32[]{:S(2)}) async-start(s8[14680064]{0:T(1024)(128)(4,1)} %bitcast.207), calls=%async_computation.6 | async-start | bytes 8388608
  114.4 7.4 %slice-start.3 = ((s8[14680064]{0:T(1024)(128)(4,1)}), s8[2097152]{0:T(1024)(128)(4,1)S(1)}, s32[]{:S(2)}) async-start(s8[14680064]{0:T(1024)(128)(4,1)} %bitcast.207), calls=%async_computation.7 | async-start | bytes 4194304
  224.5 3.1 %copy-start = (bf16[4,128,1792]{2,1,0:T(8,128)(2,1)S(1)}, bf16[4,128,1792]{2,1,0:T(8,128)(2,1)}, u32[]{:S(2)}) copy-start(bf16[4,128,1792]{2,1,0:T(8,128)(2,1)} %param.22) | copy-start | bytes 5505028
  224.6 4.8 %slice-start.4 = ((s8[4587520]{0:T(1024)(128)(4,1)}), s8[393216]{0:T(1024)(128)(4,1)S(1)}, s32[]{:S(2)}) async-start(s8[4587520]{0:T(1024)(128)(4,1)} %bitcast.209), calls=%async_computation.8 | async-start | bytes 786432
  227.7 2.2 slice-start.5
  228.5 1.4 copy-start.5
Sparse Core Ops, SparseCore 0:
  38.8 24.6 reduce-scatter.1
  65.7 35.6 all-gather.4
  162.4 50.4 all-gather.6
